TPU v7x, 1024 devices: a whole 4x4x32 slice. The times are simulated.
1024 devices in a mesh: dp: 64 (over z_lo, y, core), mp: 16 (over x, z_hi).
Axes of the slice: x: 4, y: 4, z: 32 (z_hi: 4, z_lo: 8; z = z_hi * 8 + z_lo), core: 2. Of those that a mesh axis runs over, the one named last changes fastest.
Arguments:
- attn_out: bfloat16 [16384, 3072], P('dp', 'mp'), may hold values from -6 to 6
- w_out: bfloat16 [3072, 3072], P('mp', 'dp'), may hold values from -0.109375 to 0.109375
- cotangent: bfloat16 [16384, 3072], P('dp', 'mp'), may hold values from -16 to 16
Outputs:
- projected: bfloat16 [16384, 3072], P('dp', 'mp')
- attn_grad: bfloat16 [16384, 3072], P('dp', 'mp')
- weight_grad: float32 [3072, 3072], P('mp', 'dp')
All inputs are finite; a program needn't handle non-finite values.
Results may differ from a plain program's by a relative error of at most 0.018.
Values may be sent and summed in bfloat16 or wider, within the bound.
A program may use at most 32 MiB of HBM per device.

v0:
```python
import jax
import jax.numpy as jnp
from jax import lax
from jax.sharding import PartitionSpec as P


def on_device(attn_out, w_out, cotangent):
    w_rows = lax.all_gather(w_out, "dp", axis=1, tiled=True)
    partial_sum = jnp.dot(attn_out, w_rows, preferred_element_type=jnp.float32)
    projected = lax.psum_scatter(
        partial_sum.astype(jnp.bfloat16), "mp", scatter_dimension=1, tiled=True
    )
    piece = lax.all_gather(cotangent, "mp", axis=1, tiled=True)
    running = lax.dot_general(
        piece, w_rows, (((1,), (1,)), ((), ())), preferred_element_type=jnp.float32
    )
    grad_block = lax.dot_general(
        attn_out, piece, (((0,), (0,)), ((), ())), preferred_element_type=jnp.float32
    )
    grad_blocks = grad_block
    attn_sum, grad_blocks = (running, grad_blocks)
    weight_grad = lax.psum_scatter(grad_blocks, "dp", scatter_dimension=1, tiled=True)
    return (projected, attn_sum.astype(jnp.bfloat16), weight_grad)


def solution(mesh):
    return jax.shard_map(
        on_device,
        mesh=mesh,
        in_specs=(P("dp", "mp"), P("mp", "dp"), P("dp", "mp")),
        out_specs=(P("dp", "mp"), P("dp", "mp"), P("mp", "dp")),
        check_vma=False,
    )
```

profile of v0, /device:TPU:2, one launch (start us, length us, event | category | flops | bytes accessed | tf_op | source)
XLA Modules:
  0.0 947.8 jit_solution(3659401318925638021)
XLA Ops:
  7.2 0.0 copy-start
  7.2 0.0 all-gather.3.cloned.1.call-start
  7.2 0.7 all-gather.3.cloned.1.call-update
  7.9 0.0 all-gather.5.cloned.1.call-start
  8.0 0.7 all-gather.5.cloned.1.call-update
  8.7 0.0 reduce-scatter.3.cloned.1.call-start
  8.7 140.1 %all-gather.3.cloned.1.call-done = bf16[192,3072]{0,1:T(8,128)(2,1)} async-done(((bf16[192,48]{0,1:T(8,128)(2,1)}), bf16[192,3072]{0,1:T(8,128)(2,1)}) %all-gather.3.cloned.1.call-update) | async-done | bytes 1179664 | tf_op jit(solution)/shard_map/all_gather | solution.py:8
  148.8 0.0 copy-done
  148.8 3.1 convolution_convert_fusion
  152.0 0.0 reduce-scatter.3.cloned.1.call-update
  152.0 0.0 reduce-scatter.5.cloned.1.call-start
  152.0 143.0 %all-gather.5.cloned.1.call-done = bf16[256,3072]{0,1:T(8,128)(2,1)} async-done(((bf16[256,192]{0,1:T(8,128)(2,1)}), bf16[256,3072]{0,1:T(8,128)(2,1)}) %all-gather.5.cloned.1.call-update) | async-done | bytes 1572880 | tf_op jit(solution)/shard_map/all_gather | solution.py:13
  295.0 3.6 fusion
  298.6 0.0 copy-start.1
  298.6 0.0 copy-start.2
  298.6 0.0 reduce-scatter.5.cloned.1.call-update
  298.7 1.4 copy-done.1
  300.0 0.5 copy-done.2
  300.5 1.3 convolution_convert_fusion.1
  301.9 194.0 %reduce-scatter.3.cloned.1.call-done = bf16[256,192]{0,1:T(8,128)(2,1)} async-done(((bf16[256,3072]{0,1:T(8,128)(2,1)}), bf16[256,192]{0,1:T(8,128)(2,1)}) %reduce-scatter.3.cloned.1.call-update) | async-done | bytes 98320 | tf_op jit(solution)/shard_map/reduce_scatter | solution.py:10
  495.9 445.4 %reduce-scatter.5.cloned.1.call-done = f32[192,48]{0,1:T(8,128)} async-done(((f32[192,3072]{0,1:T(8,128)}), f32[192,48]{0,1:T(8,128)}) %reduce-scatter.5.cloned.1.call-update) | async-done | bytes 36880 | tf_op jit(solution)/shard_map/reduce_scatter | solution.py:22
Async XLA Ops:
  7.2 141.7 %copy-start = (bf16[256,192]{0,1:T(8,128)(2,1)S(1)}, bf16[256,192]{0,1:T(8,128)(2,1)}, u32[]{:S(2)}) copy-start(bf16[256,192]{0,1:T(8,128)(2,1)} %param.3) | copy-start | bytes 294916
  7.2 141.7 %all-gather.3.cloned.1.call-start = ((), (), s32[]{:S(2)}) async-start(), calls=%async_computation.2 | async-start | bytes 1597440 | tf_op jit(solution)/shard_map/all_gather | solution.py:8
  7.9 287.1 %all-gather.5.cloned.1.call-start = ((), (), s32[]{:S(2)}) async-start(), calls=%async_computation.4 | async-start | bytes 1671168 | tf_op jit(solution)/shard_map/all_gather | solution.py:13
  8.7 487.2 %reduce-scatter.3.cloned.1.call-start = ((), (), s32[]{:S(2)}) async-start(), calls=%async_computation.3 | async-start | bytes 1671168 | tf_op jit(solution)/shard_map/reduce_scatter | solution.py:10
  152.0 789.3 %reduce-scatter.5.cloned.1.call-start = ((), (), s32[]{:S(2)}) async-start(), calls=%async_computation.5 | async-start | bytes 3194880 | tf_op jit(solution)/shard_map/reduce_scatter | solution.py:22
  298.6 1.4 copy-start.1
  298.6 1.9 copy-start.2
Sparse Core Ops, SparseCore 0:
  10.7 138.0 all-gather.2
  153.1 141.8 all-gather.4
  300.8 194.9 reduce-scatter.2
  499.7 441.5 reduce-scatter.4
where the time goes:
time: 948 us
  waiting for transfers between devices  924 us (97%)
  between operations  13.8 us (1%)
    reduce_scatter x1, waiting for transfers between devices, on_device(): lax.psum_scatter(grad_blocks, 'dp', scatter_dimension=1, tiled=True)  445 us
    reduce_scatter x1, waiting for transfers between devices, on_device(): lax.psum_scatter(partial_sum.astype(jnp.bfloat16), 'mp', scatter_dimensio...  194 us
    all_gather x1, waiting for transfers between devices, on_device(): piece = lax.all_gather(cotangent, 'mp', axis=1, tiled=True)  143 us
    all_gather x1, waiting for transfers between devices, on_device(): w_rows = lax.all_gather(w_out, 'dp', axis=1, tiled=True)  140 us
  transfers between devices with their start and end apart: 4, of which 4 were waited for; matrix products, arithmetic and copies ran while one was open for 1% of the time, Pallas kernels for 0%

commit v1 on v0

v1 whole, which is shorter than its diff:
```python
import functools

import jax
import jax.numpy as jnp
from jax import lax
from jax.experimental import pallas as pl
from jax.experimental.pallas import tpu as pltpu
from jax.sharding import PartitionSpec as P

BF16 = jnp.bfloat16
F32 = jnp.float32
CHUNKS = 2
LANES = 128
BLOCK = 192
SHARD = 48


def flip1(a):
    return a + 1 - 2 * (a % 2)


def flip2(a):
    return a + 2 - 4 * ((a // 2) % 2)


def flip4(a):
    return a + 4 - 8 * ((a // 4) % 2)


class Wire:
    def __init__(self, sems, index, src, dst, device):
        self.copy = pltpu.make_async_remote_copy(
            src_ref=src,
            dst_ref=dst,
            send_sem=sems[0].at[index],
            recv_sem=sems[1].at[index],
            device_id=device,
            device_id_type=pl.DeviceIdType.MESH,
        )

    def start(self):
        self.copy.start()
        return self

    def got(self):
        self.copy.wait_recv()

    def sent(self):
        self.copy.wait_send()


N_WIRES = 96


def kernel(
    x_ref, w_ref, g_ref,
    proj_ref, agrad_ref, wgrad_ref,
    xt, ct, wbuf, wown, wgot, wn,
    fpart, fgot, fsend, fzgot,
    bsend, bzgot, bown,
    gbuf, ggot, hbuf, hgot, ibuf, igot3, igot2, igot1, asend, agot,
    send_sem, recv_sem,
):
    sems = (send_sem, recv_sem)
    counter = [0]
    dp = lax.axis_index("dp")
    mp = lax.axis_index("mp")
    x, zh = mp // 4, mp % 4
    zl, y, core = dp // 8, (dp // 2) % 4, dp % 2

    def device(x=x, zh=zh, zl=zl, y=y, core=core):
        return ((zl * 4 + y) * 2 + core, x * 4 + zh)

    def wire(src, dst, to):
        counter[0] += 1
        return Wire(sems, counter[0] - 1, src, dst, to)

    near = device(zh=flip1(zh))
    far = device(zh=3 - zh)
    other = device(core=1 - core)
    x_to = [(x + d) % 4 for d in range(4)]
    y_to = [(y + d) % 4 for d in range(4)]
    l1, l2, l4 = device(zl=flip1(zl)), device(zl=flip2(zl)), device(zl=flip4(zl))

    barrier = pltpu.get_barrier_semaphore()
    partners = [near, far, other, l1, l2, l4]
    partners += [device(x=x_to[d]) for d in (1, 2, 3)]
    partners += [device(y=y_to[d]) for d in (1, 2, 3)]
    for partner in partners:
        pl.semaphore_signal(
            barrier, inc=1, device_id=partner, device_id_type=pl.DeviceIdType.MESH
        )

    za, zb = zh // 2, zh % 2

    def place(yy):
        return (yy // 2 + zb) % 2, yy % 2

    sel, half = place(y)
    keeps = (zl % 2) == ((za + sel) % 2)
    gives = (zl % 2) != ((za + sel) % 2)
    k = zl // 2

    xt_all = x_ref[...].T
    ct_all = g_ref[...].T
    for c in range(CHUNKS):
        xt[c, 0] = xt_all[:, c * LANES:(c + 1) * LANES]
        ct[c, x, 0] = ct_all[:, c * LANES:(c + 1) * LANES]
    wown[...] = w_ref[...].T

    pl.semaphore_wait(barrier, len(partners))

    w_a = wire(wown, wgot, near)

    @pl.when(gives)
    def _():
        w_a.start()

    zx = [wire(xt.at[c, 0], xt.at[c, 1], near).start() for c in range(CHUNKS)]
    zc = [wire(ct.at[c, x, 0], ct.at[c, x, 1], far).start() for c in range(CHUNKS)]
    xc0 = [
        [wire(ct.at[c, x, 0], ct.at[c, x, 0], device(x=x_to[d])).start() for d in (1, 2, 3)]
        for c in range(CHUNKS)
    ]
    xc1 = [
        [wire(ct.at[c, x, 1], ct.at[c, x, 1], device(x=x_to[d])) for d in (1, 2, 3)]
        for c in range(CHUNKS)
    ]

    def segment(kk):
        return wbuf.at[kk, sel, half, core]

    column = wbuf.at[:, sel, half, core]
    w_b1 = wire(segment(k), segment(k), l4)
    w_b2 = [wire(segment(kk), segment(kk), l2) for kk in (k, flip2(k))]
    w_b3 = wire(column, column, l1)
    w_c = [wire(column, column, device(y=y_to[d])) for d in (1, 2, 3)]

    @pl.when(keeps)
    def _():
        w_a.got()
        wbuf[k, sel, half, core] = jnp.concatenate([wown[...], wgot[...]], axis=1)
        w_b1.start()
        w_b1.got()
        for w in w_b2:
            w.start()
        for w in w_b2:
            w.got()
        w_b3.start()

    @pl.when(gives)
    def _():
        w_b3.got()

    for w in w_c:
        w.start()

    for c in range(CHUNKS):
        zc[c].got()
        for w in xc1[c]:
            w.start()

    w_d = []
    for d in range(4):
        if d:
            w_c[d - 1].got()
        s, h = place((y + 4 - d) % 4)
        part = wbuf.at[:, s, h, core]
        w_d.append(wire(part, part, other).start())
    for w in w_d:
        w.got()

    rows = 2 * BLOCK
    for kk in range(4):
        wn[:, kk * rows:(kk + 1) * rows] = wbuf[kk].reshape(rows, rows).T

    f_x, f_z, b_z = [], [], []
    for c in range(CHUNKS):
        zx[c].got()
        xval = xt[c].reshape(rows, LANES)
        for kk in range(4):
            part = jnp.dot(wbuf[kk].reshape(rows, rows), xval, preferred_element_type=F32)
            fpart[c, kk] = part.astype(BF16).reshape(2, BLOCK, LANES)
        f_x.append([
            wire(fpart.at[c, x_to[d]], fgot.at[c, d - 1], device(x=x_to[d])).start()
            for d in (1, 2, 3)
        ])
    for c in range(CHUNKS):
        for w in xc0[c] + xc1[c]:
            w.got()
        part = jnp.dot(wn[...], ct[c].reshape(4 * rows, LANES), preferred_element_type=F32)
        bown[c] = part[:BLOCK]
        bsend[c] = part[BLOCK:].astype(BF16)
        b_z.append(wire(bsend.at[c], bzgot.at[c], near).start())
        for w in f_x[c]:
            w.got()
        total = fpart[c, x].astype(F32)
        for d in range(3):
            total += fgot[c, d].astype(F32)
        fsend[c] = total[1].astype(BF16)
        f_z.append(wire(fsend.at[c], fzgot.at[c], far).start())
        fpart[c, x, 0] = total[0].astype(BF16)

    g_d = []
    for kk in range(4):
        part = jnp.zeros((rows, rows), F32)
        for c in range(CHUNKS):
            part += lax.dot_general(
                ct[c, kk].reshape(rows, LANES), xt[c].reshape(rows, LANES),
                (((1,), (1,)), ((), ())), preferred_element_type=F32,
            )
        gbuf[kk] = part.astype(BF16).reshape(2, 2, 2, SHARD, rows)
        g_d.append(wire(gbuf.at[kk, :, :, 1 - core], ggot.at[kk], other).start())
    for kk in range(4):
        g_d[kk].got()
        hbuf[:, :, kk] = (gbuf[kk, :, :, core].astype(F32) + ggot[kk].astype(F32)).astype(BF16)
    g_c = []
    for d in (1, 2, 3):
        s, h = place(y_to[d])
        g_c.append(wire(hbuf.at[s, h], hgot.at[d - 1], device(y=y_to[d])).start())
    for w in g_c:
        w.got()
    total = hbuf[sel, half].astype(F32)
    for d in range(3):
        total += hgot[d].astype(F32)
    ibuf[...] = total.astype(BF16)
    g_b3 = wire(ibuf, igot3, l1)
    g_b2 = [wire(ibuf.at[kk], igot2.at[i], l2) for i, kk in enumerate((flip1(k), 3 - k))]
    g_b1 = wire(ibuf.at[flip2(k)], igot1, l4)
    g_a = wire(asend, agot, near)

    @pl.when(gives)
    def _():
        g_b3.start()
        g_a.got()
        wgrad_ref[...] = agot[...].astype(F32)

    @pl.when(keeps)
    def _():
        g_b3.got()
        ibuf[...] = (ibuf[...].astype(F32) + igot3[...].astype(F32)).astype(BF16)
        for w in g_b2:
            w.start()
        for w in g_b2:
            w.got()
        for i, kk in enumerate((k, flip2(k))):
            ibuf[kk] = (ibuf[kk].astype(F32) + igot2[i].astype(F32)).astype(BF16)
        g_b1.start()
        g_b1.got()
        done = ibuf[k].astype(F32) + igot1[...].astype(F32)
        asend[...] = done[:, BLOCK:].astype(BF16)
        g_a.start()
        wgrad_ref[...] = done[:, :BLOCK]

    for c in range(CHUNKS):
        f_z[c].got()
        b_z[c].got()
        lanes = slice(c * LANES, (c + 1) * LANES)
        proj_ref[:, lanes] = (fpart[c, x, 0].astype(F32) + fzgot[c].astype(F32)).astype(BF16)
        agrad_ref[:, lanes] = (bown[c] + bzgot[c].astype(F32)).astype(BF16)

    for w in zx + zc + xc0[0] + xc0[1] + xc1[0] + xc1[1] + w_c + w_d:
        w.sent()
    for w in f_x[0] + f_x[1] + f_z + b_z + g_d + g_c:
        w.sent()

    @pl.when(gives)
    def _():
        w_a.sent()
        g_b3.sent()

    @pl.when(keeps)
    def _():
        for w in [w_b1, w_b3, g_b1, g_a] + w_b2 + g_b2:
            w.sent()

    assert counter[0] <= N_WIRES


def on_device(attn_out, w_out, cotangent):
    tokens, block = attn_out.shape
    vmem = pl.BlockSpec(memory_space=pltpu.VMEM)
    rows = 2 * BLOCK

    def buf(*shape, dtype=BF16):
        return pltpu.VMEM(shape, dtype)

    proj, agrad, wgrad = pl.pallas_call(
        kernel,
        out_shape=(
            jax.ShapeDtypeStruct((block, tokens), BF16),
            jax.ShapeDtypeStruct((block, tokens), BF16),
            jax.ShapeDtypeStruct((SHARD, BLOCK), F32),
        ),
        in_specs=[vmem] * 3,
        out_specs=(vmem,) * 3,
        scratch_shapes=[
            buf(CHUNKS, 2, BLOCK, LANES),
            buf(CHUNKS, 4, 2, BLOCK, LANES),
            buf(4, 2, 2, 2, SHARD, rows),
            buf(SHARD, BLOCK),
            buf(SHARD, BLOCK),
            buf(rows, 4 * rows),
            buf(CHUNKS, 4, 2, BLOCK, LANES),
            buf(CHUNKS, 3, 2, BLOCK, LANES),
            buf(CHUNKS, BLOCK, LANES),
            buf(CHUNKS, BLOCK, LANES),
            buf(CHUNKS, BLOCK, LANES),
            buf(CHUNKS, BLOCK, LANES),
            buf(CHUNKS, BLOCK, LANES, dtype=F32),
            buf(4, 2, 2, 2, SHARD, rows),
            buf(4, 2, 2, SHARD, rows),
            buf(2, 2, 4, SHARD, rows),
            buf(3, 4, SHARD, rows),
            buf(4, SHARD, rows),
            buf(4, SHARD, rows),
            buf(2, SHARD, rows),
            buf(SHARD, rows),
            buf(SHARD, BLOCK),
            buf(SHARD, BLOCK),
            pltpu.SemaphoreType.DMA((N_WIRES,)),
            pltpu.SemaphoreType.DMA((N_WIRES,)),
        ],
        compiler_params=pltpu.CompilerParams(
            collective_id=0, has_side_effects=True, vmem_limit_bytes=48 * 2**20
        ),
    )(attn_out, w_out, cotangent)
    return proj.T, agrad.T, wgrad.T


def solution(mesh):
    return jax.shard_map(
        on_device,
        mesh=mesh,
        in_specs=(P("dp", "mp"), P("mp", "dp"), P("dp", "mp")),
        out_specs=(P("dp", "mp"), P("dp", "mp"), P("mp", "dp")),
        check_vma=False,
    )
```

time: 948 us -> 115 us (0.12)
  the two profiles are of different devices: /device:TPU:2 before, /device:TPU:32 now
where the time goes in v1:
time: 115 us
  Pallas kernels  111 us (97%)
  local copies, waits for them, and re-layouts  3.88 us (3%)
    pallas_call x1, Pallas kernels, on_device(): pl.pallas_call(kernel, out_shape=(jax.ShapeDtypeStruct((block, tokens), B...  111 us
    unnamed x8, local copies, waits for them, and re-layouts  3.88 us

profile of v1, /device:TPU:32, one launch (start us, length us, event | category | flops | bytes accessed | tf_op | source)
XLA Modules:
  0.0 115.1 jit_solution(3217888809660691416)
XLA Ops:
  0.6 0.8 copy.7.w_ref
  1.5 0.0 copy-start
  1.5 1.0 copy.6.x_ref
  2.5 0.0 copy-done
  2.5 0.1 copy.8.g_ref
  2.6 110.6 %shard_map.58 = (bf16[192,256]{1,0:T(8,128)(2,1)S(1)}, bf16[192,256]{1,0:T(8,128)(2,1)S(1)}, f32[48,192]{1,0:T(8,128)S(1)}) custom-call(bf16[256,192]{1,0:T(8,128)(2,1)S(1)} %copy.6.x_ref, bf16[192,48]{1,0:T(8,128)(2,1)S(1)} %copy.7.w_ref, bf16[256,192]{1,0:T(8,128)(2,1)S(1)} %copy.8.g_ref), custom_call_target="tpu_custom_call" | custom-call | tf_op jit(solution)/shard_map/pallas_call | solution.py:288
  113.2 0.6 copy.12
  113.9 0.6 copy.13
  114.5 0.6 copy.14
Async XLA Ops:
  1.5 1.0 copy-start

commit v2 on v0

v2 whole, which is shorter than its diff:
```python
import jax
import jax.numpy as jnp
from jax import lax
from jax.experimental import pallas as pl
from jax.experimental.pallas import tpu as pltpu
from jax.sharding import PartitionSpec as P

BF16 = jnp.bfloat16
F32 = jnp.float32
CHUNKS = 2
LANES = 128
BLOCK = 192
SHARD = 48


def flip1(a):
    return a + 1 - 2 * (a % 2)


def flip4(a):
    return a + 4 - 8 * ((a // 4) % 2)


class Wire:
    def __init__(self, sems, index, arrives, src, dst, device):
        self.copy = pltpu.make_async_remote_copy(
            src_ref=src,
            dst_ref=dst,
            send_sem=sems[0].at[index],
            recv_sem=sems[1].at[arrives],
            device_id=device,
            device_id_type=pl.DeviceIdType.MESH,
        )
        self.leaves = False

    def start(self, only=None):
        self.leaves = True if only is None else only
        if only is None:
            self.copy.start()
        else:
            pl.when(only)(self.copy.start)
        return self

    def got(self, only=None):
        if only is None:
            self.copy.wait_recv()
        else:
            pl.when(only)(self.copy.wait_recv)

    def sent(self):
        if self.leaves is True:
            self.copy.wait_send()
        elif self.leaves is not False:
            pl.when(self.leaves)(self.copy.wait_send)


N_WIRES = 96
VMEM_LIMIT = 64 * 2**20 - 2**16


def kernel(
    x_ref, w_ref, g_ref,
    proj_ref, agrad_ref, wgrad_ref,
    xin, gin, xt, ct, wbuf, wown, wgot, wn,
    fpart, fgot, fsend, fzgot,
    bsend, bzgot, bown,
    gbuf, ggot, hbuf, hgot, ibuf, igot, tot, asend, agot,
    load_sem, send_sem, recv_sem,
):
    sems = (send_sem, recv_sem)
    counter, wires = [0], []
    dp = lax.axis_index("dp")
    mp = lax.axis_index("mp")
    x, zh = mp // 4, mp % 4
    zl, y, core = dp // 8, (dp // 2) % 4, dp % 2

    def device(x=x, zh=zh, zl=zl, y=y, core=core):
        return ((zl * 4 + y) * 2 + core, x * 4 + zh)

    def wire(src, dst, to, arrives=None):
        counter[0] += 1
        index = counter[0] - 1
        wires.append(Wire(sems, index, index if arrives is None else arrives, src, dst, to))
        return wires[-1]

    def reserve(n):
        counter[0] += n
        return counter[0] - n

    zn = flip1(zh)
    near, far, other = device(zh=zn), device(zh=3 - zh), device(core=1 - core)
    zl4 = flip4(zl)
    l4, near4 = device(zl=zl4), device(zh=zn, zl=zl4)
    x_to = [(x + d) % 4 for d in range(4)]
    y_to = [(y + d) % 4 for d in range(4)]
    pos, line = zl % 4, (zl // 4) * 4
    z_to = [device(zl=line + (pos + d) % 4) for d in range(4)]

    barrier = pltpu.get_barrier_semaphore()
    partners = [near, far, other, l4, near4] + z_to[1:]
    partners += [device(x=x_to[d]) for d in (1, 2, 3)]
    partners += [device(y=y_to[d]) for d in (1, 2, 3)]
    for partner in partners:
        pl.semaphore_signal(
            barrier, inc=1, device_id=partner, device_id_type=pl.DeviceIdType.MESH
        )

    loads = [
        pltpu.make_async_copy(src, dst, load_sem.at[i])
        for i, (src, dst) in enumerate(((x_ref, xin), (g_ref, gin), (w_ref, wown)))
    ]
    for load in loads:
        load.start()

    za, zb = zh // 2, zh % 2

    def place(yy):
        return (yy // 2 + zb) % 2, yy % 2

    def parity(yy):
        return (za + place(yy)[0]) % 2

    def first(yy):
        away = (zl + parity(yy)) % 2
        return ((pos + 3 * away) % 4) // 2

    sel, half = place(y)
    par = parity(y)
    keeps = (zl % 2) == par
    gives = (zl % 2) != par
    khi, klo = zl // 4, (zl // 2) % 2

    for load in loads:
        load.wait()
    for c in range(CHUNKS):
        xt[c, 0] = xin[:, c * LANES:(c + 1) * LANES]
        ct[c, x, 0] = gin[:, c * LANES:(c + 1) * LANES]

    pl.semaphore_wait(barrier, len(partners))

    w_a = [wire(wown, wgot.at[i], to) for i, to in enumerate((near, near4, l4))]

    zx = [wire(xt.at[c, 0], xt.at[c, 1], near) for c in range(CHUNKS)]
    zc = [wire(ct.at[c, x, 0], ct.at[c, x, 1], far) for c in range(CHUNKS)]
    xc0 = [
        [wire(ct.at[c, x, 0], ct.at[c, x, 0], device(x=x_to[d])) for d in (1, 2, 3)]
        for c in range(CHUNKS)
    ]
    xc1 = [
        [wire(ct.at[c, x, 1], ct.at[c, x, 1], device(x=x_to[d])) for d in (1, 2, 3)]
        for c in range(CHUNKS)
    ]

    def pair(low, yy):
        s, h = place(yy)
        return wbuf.at[:, low, s, h, core]

    one = first(y)
    lows = (one, 1 - one)
    w_b = [None] + [wire(pair(klo, y), pair(klo, y), z_to[d]) for d in (1, 2, 3)]
    w_c = [
        [wire(pair(low, y), pair(low, y), device(y=y_to[d])) for d in (1, 2, 3)]
        for low in lows
    ]
    w_d = [[], []]
    for d in range(4):
        yy = (y + 4 - d) % 4
        for i in range(2):
            low = first(yy) if i == 0 else 1 - first(yy)
            w_d[i].append(wire(pair(low, yy), pair(low, yy), other))

    def weights_a():
        w_a[0].start(gives)
        w_a[1].start(gives)
        w_a[2].start(keeps)

    def weights_line():
        @pl.when(keeps)
        def _():
            for w in w_a:
                w.got()
            wbuf[khi, klo, sel, half, core] = jnp.concatenate([wown[...], wgot[0]], axis=1)
            wbuf[1 - khi, klo, sel, half, core] = jnp.concatenate([wgot[2], wgot[1]], axis=1)

        for d in (1, 3, 2):
            w_b[d].start(keeps)

    def weights_y(i):
        if i == 0:
            w_b[1].got(gives)
        else:
            w_b[2].got(keeps)
            w_b[3].got(gives)
        for w in w_c[i] + [w_d[i][0]]:
            w.start()

    def weights_core(i):
        for d in (1, 2, 3):
            w_c[i][d - 1].got()
            w_d[i][d].start()

    def weights_end():
        for i in range(2):
            for d in range(4):
                w_d[i][d].got()
        for kk in range(4):
            wn[:, kk * rows:(kk + 1) * rows] = weights(kk).T

    def gather_z(c, only=None):
        zx[c].start(only)
        zc[c].start(only)

    def gather_x0():
        for c in range(CHUNKS):
            for w in xc0[c]:
                w.start()

    def gather_x1(c):
        zc[c].got()
        for w in xc1[c]:
            w.start()

    rows = 2 * BLOCK

    def weights(kk):
        return wbuf[kk // 2, kk % 2].reshape(rows, rows)

    f_x, f_z, b_z = [], [], []

    def gathered(c):
        zx[c].got()
        for w in xc0[c] + xc1[c]:
            w.got()

    def forward(c):
        xval = xt[c].reshape(rows, LANES)
        for kk in range(4):
            part = jnp.dot(weights(kk), xval, preferred_element_type=F32)
            fpart[c, kk] = part.astype(BF16).reshape(2, BLOCK, LANES)
        f_x.append([
            wire(fpart.at[c, x_to[d]], fgot.at[c, d - 1], device(x=x_to[d])).start()
            for d in (1, 2, 3)
        ])

    def backward(c):
        part = jnp.dot(wn[...], ct[c].reshape(4 * rows, LANES), preferred_element_type=F32)
        bown[c] = part[:BLOCK]
        bsend[c] = part[BLOCK:].astype(BF16)
        b_z.append(wire(bsend.at[c], bzgot.at[c], near))

    def forward_sum(c):
        for w in f_x[c]:
            w.got()
        total = fpart[c, x].astype(F32)
        for d in range(3):
            total += fgot[c, d].astype(F32)
        fsend[c] = total[1].astype(BF16)
        f_z.append(wire(fsend.at[c], fzgot.at[c], far))
        fpart[c, x, 0] = total[0].astype(BF16)

    g_d = [None] * 4

    def gradient(low):
        for kk in (low, low + 2):
            part = jnp.zeros((rows, rows), F32)
            for c in range(CHUNKS):
                part += lax.dot_general(
                    ct[c, kk].reshape(rows, LANES), xt[c].reshape(rows, LANES),
                    (((1,), (1,)), ((), ())), preferred_element_type=F32,
                )
            gbuf[kk] = part.astype(BF16).reshape(2, 2, 2, SHARD, rows)
            g_d[kk] = wire(gbuf.at[kk, :, :, 1 - core], ggot.at[kk], other).start()

    g_c = [[], []]

    def gradient_y(low):
        for i in range(2):
            kk = low + 2 * i
            g_d[kk].got()
            hbuf[low, :, :, i] = (
                gbuf[kk, :, :, core].astype(F32) + ggot[kk].astype(F32)
            ).astype(BF16)
        for d in (1, 2, 3):
            s, h = place(y_to[d])
            g_c[low].append(
                wire(hbuf.at[low, s, h], hgot.at[low, d - 1], device(y=y_to[d])).start()
            )

    g_b_base = reserve(3)
    g_b = [None, None]

    def gradient_z(low):
        for w in g_c[low]:
            w.got()
        total = hbuf[low, sel, half].astype(F32)
        for d in range(3):
            total += hgot[low, d].astype(F32)
        ibuf[low] = total.astype(BF16)
        goal = 2 * low + par
        step = (goal + 4 - pos) % 4
        slot = (step + 3) % 4
        slot = slot - slot // 3
        g_b[low] = wire(ibuf.at[low], igot.at[slot], device(zl=line + goal), g_b_base + slot)
        g_b[low].start(step != 0)

    g_b_in = [wire(ibuf.at[0], igot.at[d], other, g_b_base + d) for d in range(3)]
    g_a = [wire(asend.at[i], agot.at[i], to) for i, to in enumerate((near, near4, l4))]

    def gradient_sum():
        @pl.when(keeps)
        def _():
            for w in g_b_in:
                w.got()
            total = ibuf[klo].astype(F32)
            for d in range(3):
                total += igot[d].astype(F32)
            tot[...] = total
            asend[0] = tot[khi][:, BLOCK:].astype(BF16)
            asend[1] = tot[1 - khi][:, BLOCK:].astype(BF16)
            asend[2] = tot[1 - khi][:, :BLOCK].astype(BF16)

        for w in (g_a[1], g_a[0], g_a[2]):
            w.start(keeps)

    def gradient_end():
        @pl.when(keeps)
        def _():
            g_a[2].got()
            wgrad_ref[...] = tot[khi][:, :BLOCK] + agot[2].astype(F32)

        @pl.when(gives)
        def _():
            g_a[0].got()
            g_a[1].got()
            wgrad_ref[...] = agot[0].astype(F32) + agot[1].astype(F32)

    def finish(c):
        f_z[c].got()
        b_z[c].got()
        lanes = slice(c * LANES, (c + 1) * LANES)
        proj_ref[:, lanes] = (fpart[c, x, 0].astype(F32) + fzgot[c].astype(F32)).astype(BF16)
        agrad_ref[:, lanes] = (bown[c] + bzgot[c].astype(F32)).astype(BF16)

    weights_a()
    gather_z(0)
    gather_z(1)
    gather_x0()
    weights_line()
    weights_y(0)
    gather_x1(0)
    weights_y(1)
    gather_x1(1)
    weights_core(0)
    weights_core(1)
    gathered(0)
    gathered(1)
    gradient(0)
    gradient(1)
    weights_end()
    backward(0)
    b_z[0].start()
    forward(0)
    gradient_y(0)
    gradient_y(1)
    forward_sum(0)
    f_z[0].start()
    backward(1)
    forward(1)
    gradient_z(0)
    gradient_z(1)
    b_z[1].start()
    forward_sum(1)
    f_z[1].start()
    gradient_sum()
    finish(0)
    finish(1)
    gradient_end()

    for w in wires:
        w.sent()

    assert counter[0] <= N_WIRES


def on_device(attn_out, w_out, cotangent):
    tokens, block = attn_out.shape
    vmem = pl.BlockSpec(memory_space=pltpu.VMEM)
    rows = 2 * BLOCK

    def buf(*shape, dtype=BF16):
        return pltpu.VMEM(shape, dtype)

    proj, agrad, wgrad = pl.pallas_call(
        kernel,
        out_shape=(
            jax.ShapeDtypeStruct((block, tokens), BF16),
            jax.ShapeDtypeStruct((block, tokens), BF16),
            jax.ShapeDtypeStruct((SHARD, BLOCK), F32),
        ),
        in_specs=[pl.BlockSpec(memory_space=pltpu.HBM)] * 3,
        out_specs=(vmem,) * 3,
        scratch_shapes=[
            buf(BLOCK, tokens),
            buf(BLOCK, tokens),
            buf(CHUNKS, 2, BLOCK, LANES),
            buf(CHUNKS, 4, 2, BLOCK, LANES),
            buf(2, 2, 2, 2, 2, SHARD, rows),
            buf(SHARD, BLOCK),
            buf(3, SHARD, BLOCK),
            buf(rows, 4 * rows),
            buf(CHUNKS, 4, 2, BLOCK, LANES),
            buf(CHUNKS, 3, 2, BLOCK, LANES),
            buf(CHUNKS, BLOCK, LANES),
            buf(CHUNKS, BLOCK, LANES),
            buf(CHUNKS, BLOCK, LANES),
            buf(CHUNKS, BLOCK, LANES),
            buf(CHUNKS, BLOCK, LANES, dtype=F32),
            buf(4, 2, 2, 2, SHARD, rows),
            buf(4, 2, 2, SHARD, rows),
            buf(2, 2, 2, 2, SHARD, rows),
            buf(2, 3, 2, SHARD, rows),
            buf(2, 2, SHARD, rows),
            buf(3, 2, SHARD, rows),
            buf(2, SHARD, rows, dtype=F32),
            buf(3, SHARD, BLOCK),
            buf(3, SHARD, BLOCK),
            pltpu.SemaphoreType.DMA((3,)),
            pltpu.SemaphoreType.DMA((N_WIRES,)),
            pltpu.SemaphoreType.DMA((N_WIRES,)),
        ],
        compiler_params=pltpu.CompilerParams(
            collective_id=0, has_side_effects=True, vmem_limit_bytes=VMEM_LIMIT
        ),
    )(attn_out.T, w_out.T, cotangent.T)
    return proj.T, agrad.T, wgrad.T


def solution(mesh):
    return jax.shard_map(
        on_device,
        mesh=mesh,
        in_specs=(P("dp", "mp"), P("mp", "dp"), P("dp", "mp")),
        out_specs=(P("dp", "mp"), P("dp", "mp"), P("mp", "dp")),
        check_vma=False,
    )
```

time: 948 us -> 104 us (0.11)
  the two profiles are of different devices: /device:TPU:2 before, /device:TPU:96 now
where the time goes in v2:
time: 104 us
  Pallas kernels  100 us (96%)
  local copies, waits for them, and re-layouts  2.99 us (3%)
    pallas_call x1, Pallas kernels, on_device(): pl.pallas_call(kernel, out_shape=(jax.ShapeDtypeStruct((block, tokens), B...  100 us
    unnamed x7, local copies, waits for them, and re-layouts  2.99 us

profile of v2, /device:TPU:96, one launch (start us, length us, event | category | flops | bytes accessed | tf_op | source)
XLA Modules:
  0.0 103.8 jit_solution(6341304169557290889)
XLA Ops:
  0.6 100.1 %shard_map.58 = (bf16[192,256]{1,0:T(8,128)(2,1)}, bf16[192,256]{1,0:T(8,128)(2,1)}, f32[48,192]{1,0:T(8,128)}) custom-call(bf16[192,256]{1,0:T(8,128)(2,1)} %bitcast.6, bf16[48,192]{1,0:T(8,128)(2,1)} %bitcast.11, bf16[192,256]{1,0:T(8,128)(2,1)} %bitcast.7), custom_call_target="tpu_custom_call" | custom-call | tf_op jit(solution)/shard_map/pallas_call | solution.py:393
  100.8 0.0 copy-start
  100.8 1.6 %copy.9 = bf16[256,192]{0,1:T(8,128)(2,1)} copy(bf16[256,192]{0,1:T(8,128)(2,1)} %bitcast.9) | data formatting | bytes 196608
  102.4 0.0 copy-done
  102.4 0.0 copy-start.1
  102.4 0.6 copy.10
  103.0 0.2 copy-done.1
  103.2 0.6 copy.11
Async XLA Ops:
  100.8 1.6 %copy-start = (bf16[192,256]{1,0:T(8,128)(2,1)S(1)}, bf16[192,256]{1,0:T(8,128)(2,1)}, u32[]{:S(2)}) copy-start(bf16[192,256]{1,0:T(8,128)(2,1)} %get-tuple-element.7) | copy-start | bytes 294916
  102.4 0.8 copy-start.1

commit v3 on v2

--- a/solution.py
+++ b/solution.py
@@ -357,15 +357,15 @@
     gradient(0)
     gradient(1)
     weights_end()
+    forward(0)
+    forward(1)
     backward(0)
     b_z[0].start()
-    forward(0)
     gradient_y(0)
     gradient_y(1)
     forward_sum(0)
     f_z[0].start()
     backward(1)
-    forward(1)
     gradient_z(0)
     gradient_z(1)
     b_z[1].start()

time: 104 us -> 103 us (level)
  no operation moved by 1% of the time
where the time goes in v3:
time: 103 us
  Pallas kernels  99.3 us (96%)
  local copies, waits for them, and re-layouts  2.99 us (3%)
    pallas_call x1, Pallas kernels, on_device(): pl.pallas_call(kernel, out_shape=(jax.ShapeDtypeStruct((block, tokens), B...  99.3 us
    unnamed x7, local copies, waits for them, and re-layouts  2.99 us

profile of v3, /device:TPU:96, one launch (start us, length us, event | category | flops | bytes accessed | tf_op | source)
XLA Modules:
  0.0 102.9 jit_solution(9936483472293015071)
XLA Ops:
  0.6 99.3 %shard_map.58 = (bf16[192,256]{1,0:T(8,128)(2,1)}, bf16[192,256]{1,0:T(8,128)(2,1)}, f32[48,192]{1,0:T(8,128)}) custom-call(bf16[192,256]{1,0:T(8,128)(2,1)} %bitcast.6, bf16[48,192]{1,0:T(8,128)(2,1)} %bitcast.11, bf16[192,256]{1,0:T(8,128)(2,1)} %bitcast.7), custom_call_target="tpu_custom_call" | custom-call | tf_op jit(solution)/shard_map/pallas_call | solution.py:393
  99.9 0.0 copy-start
  99.9 1.6 %copy.9 = bf16[256,192]{0,1:T(8,128)(2,1)} copy(bf16[256,192]{0,1:T(8,128)(2,1)} %bitcast.9) | data formatting | bytes 196608
  101.5 0.0 copy-done
  101.5 0.0 copy-start.1
  101.5 0.6 copy.10
  102.1 0.2 copy-done.1
  102.3 0.6 copy.11
Async XLA Ops:
  99.9 1.6 %copy-start = (bf16[192,256]{1,0:T(8,128)(2,1)S(1)}, bf16[192,256]{1,0:T(8,128)(2,1)}, u32[]{:S(2)}) copy-start(bf16[192,256]{1,0:T(8,128)(2,1)} %get-tuple-element.7) | copy-start | bytes 294916
  101.5 0.8 copy-start.1

commit v4 on v3

--- a/solution.py
+++ b/solution.py
@@ -366,10 +366,10 @@
     forward_sum(0)
     f_z[0].start()
     backward(1)
+    forward_sum(1)
     gradient_z(0)
     gradient_z(1)
     b_z[1].start()
-    forward_sum(1)
     f_z[1].start()
     gradient_sum()
     finish(0)

time: 103 us -> 103 us (level)
  no operation moved by 1% of the time
where the time goes in v4:
time: 103 us
  Pallas kernels  99.5 us (97%)
  local copies, waits for them, and re-layouts  2.99 us (3%)
    pallas_call x1, Pallas kernels, on_device(): pl.pallas_call(kernel, out_shape=(jax.ShapeDtypeStruct((block, tokens), B...  99.5 us
    unnamed x7, local copies, waits for them, and re-layouts  2.99 us

profile of v4, /device:TPU:96, one launch (start us, length us, event | category | flops | bytes accessed | tf_op | source)
XLA Modules:
  0.0 103.2 jit_solution(11548870503143914558)
XLA Ops:
  0.6 99.5 %shard_map.58 = (bf16[192,256]{1,0:T(8,128)(2,1)}, bf16[192,256]{1,0:T(8,128)(2,1)}, f32[48,192]{1,0:T(8,128)}) custom-call(bf16[192,256]{1,0:T(8,128)(2,1)} %bitcast.6, bf16[48,192]{1,0:T(8,128)(2,1)} %bitcast.11, bf16[192,256]{1,0:T(8,128)(2,1)} %bitcast.7), custom_call_target="tpu_custom_call" | custom-call | tf_op jit(solution)/shard_map/pallas_call | solution.py:393
  100.2 0.0 copy-start
  100.2 1.6 %copy.9 = bf16[256,192]{0,1:T(8,128)(2,1)} copy(bf16[256,192]{0,1:T(8,128)(2,1)} %bitcast.9) | data formatting | bytes 196608
  101.8 0.0 copy-done
  101.8 0.0 copy-start.1
  101.8 0.6 copy.10
  102.4 0.2 copy-done.1
  102.6 0.6 copy.11
Async XLA Ops:
  100.2 1.6 %copy-start = (bf16[192,256]{1,0:T(8,128)(2,1)S(1)}, bf16[192,256]{1,0:T(8,128)(2,1)}, u32[]{:S(2)}) copy-start(bf16[192,256]{1,0:T(8,128)(2,1)} %get-tuple-element.7) | copy-start | bytes 294916
  101.8 0.8 copy-start.1
